TPU v7x, 512 devices: a whole 4x8x8 slice. The times are simulated.
512 devices in a mesh: rep: 32 (over z, y_hi, core), fsdp: 16 (over x, y_lo).
Axes of the slice: x: 4, y: 8 (y_hi: 2, y_lo: 4; y = y_hi * 4 + y_lo), z: 8, core: 2. Of those that a mesh axis runs over, the one named last changes fastest.
Arguments:
- hidden: bfloat16 [32, 2048, 4096], P('rep', 'fsdp'), may hold values from -150 to 150
- gain: bfloat16 [32, 4096], P('rep'), may hold values from 0.25 to 1.75
- value_grad: bfloat16 [32, 2048, 512], P('rep', 'fsdp'), may hold values from -6 to 6
- value_weight: bfloat16 [32, 4096, 512], P('rep', 'fsdp'), may hold values from -0.09375 to 0.09375
- outer_delta: bfloat16 [32, 4096, 512], P('rep', 'fsdp'), may hold values from -6 to 6
- momentum: float32 [4096, 512], P('fsdp'), may hold values from -6 to 6
Outputs:
- values: bfloat16 [32, 2048, 512], P('rep', 'fsdp')
- value_weight_grad: bfloat16 [32, 4096, 512], P('rep', 'fsdp')
- hidden_grad: bfloat16 [32, 2048, 4096], P('rep', 'fsdp')
- new_momentum: float32 [4096, 512], P('fsdp')
- outer_step: float32 [4096, 512], P('fsdp')
All inputs are finite; a program needn't handle non-finite values.
Results may differ from a plain program's by a relative error of at most 0.022.
Values may be sent and summed in bfloat16 or wider, within the bound.
A program may use at most 64 MiB of HBM per device.

v0:
```python
import jax
import jax.numpy as jnp
from jax import lax
from jax.sharding import PartitionSpec as P

EPSILON = 1e-05
MOMENT = 0.9
OUTER_RATE = 0.7


def outer_update(outer_delta, momentum):
    summed = lax.psum(outer_delta[0].astype(jnp.float32).astype(jnp.bfloat16), "rep").astype(
        jnp.float32
    )
    average = summed / lax.axis_size("rep")
    new_momentum = MOMENT * momentum + average
    return (new_momentum, -OUTER_RATE * (average + MOMENT * new_momentum))


def per_device(hidden, gain, value_grad, value_weight, outer_delta, momentum):
    tokens = hidden[0]
    cotangent = value_grad[0]
    weight_rows = value_weight[0]
    gain_wide = gain[0].astype(jnp.float32)
    widened = tokens.astype(jnp.float32)
    inverse_rms = lax.rsqrt(jnp.mean(widened * widened, axis=-1, keepdims=True) + EPSILON)
    scaled = widened * inverse_rms
    normed = (scaled * gain_wide).astype(jnp.bfloat16)
    own_rows = normed.shape[0]
    segment = normed
    values_sum = jnp.dot(
        segment,
        lax.all_gather(weight_rows, "fsdp", axis=0, tiled=True),
        preferred_element_type=jnp.float32,
    )
    grad_sum = jnp.einsum(
        "tv,dv->td",
        cotangent,
        lax.all_gather(weight_rows, "fsdp", axis=0, tiled=True),
        preferred_element_type=jnp.float32,
    )
    values = values_sum.astype(jnp.bfloat16)
    normed_grad = grad_sum.astype(jnp.bfloat16)
    segment = normed
    partial_value = (
        jnp.einsum("td,tv->dv", segment, cotangent, preferred_element_type=jnp.float32) / own_rows
    )
    weight_grad = lax.psum_scatter(
        lax.optimization_barrier(partial_value.astype(jnp.bfloat16))
        .astype(jnp.float32)
        .astype(jnp.bfloat16),
        "fsdp",
        scatter_dimension=0,
        tiled=True,
    )
    gated = normed_grad.astype(jnp.float32) * gain_wide
    centred = gated - scaled * jnp.mean(gated * scaled, axis=-1, keepdims=True)
    hidden_grad = (inverse_rms * centred).astype(jnp.bfloat16)
    new_momentum, outer_step = outer_update(outer_delta, momentum)
    return (values[None], weight_grad[None], hidden_grad[None], new_momentum, outer_step)


def solution(mesh):
    in_specs = (
        P("rep", "fsdp", None),
        P("rep", None),
        P("rep", "fsdp", None),
        P("rep", "fsdp", None),
        P("rep", "fsdp", None),
        P("fsdp", None),
    )
    out_specs = (
        P("rep", "fsdp", None),
        P("rep", "fsdp", None),
        P("rep", "fsdp", None),
        P("fsdp", None),
        P("fsdp", None),
    )
    return jax.shard_map(
        per_device, mesh=mesh, in_specs=in_specs, out_specs=out_specs, check_vma=False
    )
```

profile of v0, /device:TPU:1, one launch (start us, length us, event | category | flops | bytes accessed | tf_op | source)
XLA Modules:
  0.0 429.0 jit_solution(6547485904917362026)
XLA Ops:
  8.0 0.0 copy-start
  8.0 0.0 all-reduce.2.cloned.1.call-start
  8.1 0.7 all-reduce.2.cloned.1.call-update
  8.7 0.0 all-gather.3.cloned.1.call-start
  8.8 0.5 all-gather.3.cloned.1.call-update
  9.3 0.0 reduce-scatter.2.cloned.1.call-start
  9.4 0.7 mul.89
  10.1 1.5 fusion.15
  11.6 0.0 copy-done
  11.6 4.6 %multiply_convert_fusion = bf16[4096,512]{1,0:T(8,128)(2,1)} fusion(bf16[1,128,4096]{2,1,0:T(8,128)(2,1)} %param.6, f32[4096]{0:T(1024)S(1)} %bitcast.56, f32[128]{0:T(128)S(1)} %add_rsqrt_fusion, bf16[1,128,512]{2,1,0:T(8,128)(2,1)S(1)} %copy-done), kind=kOutput, calls=%fused_computation | convolution fusion | flops 543162368 | bytes 5390848 | tf_op jit(solution)/shard_map/td,tv->dv/dot_general | solution.py:46
  16.3 0.0 copy-start.3
  16.3 0.0 copy-start.1
  16.3 0.0 reduce-scatter.2.cloned.1.call-update
  16.3 396.4 %all-reduce.2.cloned.1.call-done = bf16[256,512]{1,0:T(8,128)(2,1)} async-done(((bf16[256,512]{1,0:T(8,128)(2,1)}), bf16[256,512]{1,0:T(8,128)(2,1)}) %all-reduce.2.cloned.1.call-update) | async-done | bytes 262160 | tf_op jit(solution)/shard_map/psum | solution.py:12
  412.7 0.0 copy-done.3
  412.7 2.1 add_multiply_fusion
  414.8 0.0 all-gather.3.cloned.1.call-done
  414.8 0.0 copy-done.1
  414.8 0.0 copy-start.2
  414.8 3.9 fusion.11
  418.7 0.0 copy-done.2
  418.7 1.4 fusion.21
  420.1 1.5 fusion.26
  421.6 0.0 reduce-scatter.2.cloned.1.call-done
  (2 shorter events, 0.0 us)
Async XLA Ops:
  8.0 3.6 copy-start
  8.0 404.7 %all-reduce.2.cloned.1.call-start = ((), (), s32[]{:S(2)}) async-start(), calls=%async_computation.2 | async-start | bytes 524288 | tf_op jit(solution)/shard_map/psum | solution.py:12
  8.7 406.0 %all-gather.3.cloned.1.call-start = ((), (), s32[]{:S(2)}) async-start(), calls=%async_computation.3 | async-start | bytes 4456448 | tf_op jit(solution)/shard_map/all_gather | solution.py:33
  9.3 412.3 %reduce-scatter.2.cloned.1.call-start = ((), (), s32[]{:S(2)}) async-start(), calls=%async_computation.1 | async-start | bytes 4456448 | tf_op jit(solution)/shard_map/reduce_scatter | solution.py:48
  16.3 396.5 %copy-start.3 = (f32[256,512]{1,0:T(8,128)S(1)}, f32[256,512]{1,0:T(8,128)}, u32[]{:S(2)}) copy-start(f32[256,512]{1,0:T(8,128)} %param.11) | copy-start | bytes 1572868
  16.3 398.5 %copy-start.1 = (bf16[1,128,4096]{2,1,0:T(8,128)(2,1)S(1)}, bf16[1,128,4096]{2,1,0:T(8,128)(2,1)}, u32[]{:S(2)}) copy-start(bf16[1,128,4096]{2,1,0:T(8,128)(2,1)} %param.6) | copy-start | bytes 3145732
  414.8 3.9 copy-start.2
Sparse Core Ops, SparseCore 0:
  11.7 400.9 all-reduce.1
Sparse Core Ops, SparseCore 1:
  11.3 111.9 all-gather.2
  126.5 102.9 reduce-scatter.1
where the time goes:
time: 429 us
  waiting for transfers between devices  398 us (93%)
  between operations  15.5 us (4%)
  matrix products  9.93 us (2%)
  other arithmetic  5.81 us (1%)
    psum x1, waiting for transfers between devices, outer_update(): lax.psum(outer_delta[0].astype(jnp.float32).astype(jnp.bfloat16), 'rep')  396 us
  transfers between devices with their start and end apart: 3, of which 1 were waited for; matrix products, arithmetic and copies ran while one was open for 4% of the time, Pallas kernels for 0%

commit v1 on v0

v1 whole, which is shorter than its diff:
```python
import jax
import jax.numpy as jnp
from jax import lax
from jax.experimental import pallas as pl
from jax.experimental.pallas import tpu as pltpu
from jax.sharding import PartitionSpec as P

EPSILON = 1e-05
MOMENT = 0.9
OUTER_RATE = 0.7

TOK = 128
D = 4096
KV = 512
ROWS = 256
NX = 4
NY = 4
NZ = 8
GROUP = NX * TOK
SLICE = 16

MESH = pl.DeviceIdType.MESH
F32 = jnp.float32
BF16 = jnp.bfloat16


def exchange(
    hidden, gain, value_grad, weight, delta, momentum,
    hg_out, val_out, wg_out, nm_out, os_out,
    h_v, inv_v, row_v, n_send, n_buf, vg_buf, w_buf, ng_send, ng_buf,
    v_send, v_recv, wg_acc, wg_send, wg_recv,
    d_own, d_recv, p_send, z_recv, s_own, s_recv, avg, mom_v,
    local_sem, x_send, x_recv, n_ssem, n_rsem, g_ssem, g_rsem, v_ssem, v_rsem,
    w_ssem, w_rsem, r_ssem, r_rsem, c_ssem, c_rsem, z_ssem, z_rsem, a_ssem, a_rsem,
):
    rep = lax.axis_index("rep")
    fsdp = lax.axis_index("fsdp")
    i, j = fsdp // NY, fsdp % NY
    z, core = rep // 4, rep % 2
    high = j // 2
    mid = jnp.logical_or(j == 1, j == 2)
    outer = jnp.logical_not(mid)
    is_mid = high + j % 2 - 2 * high * (j % 2)

    def along_x(d):
        return (rep, ((i + d) % NX) * NY + j)

    def along_z(d):
        return (((z + d) % NZ) * 4 + rep % 4, fsdp)

    inward = (rep, i * NY + j + 1 - 2 * high)
    outward = (rep, i * NY + j - 1 + 2 * high)
    other_core = (rep + 1 - 2 * core, fsdp)
    other_half = (rep + 2 - 4 * ((rep // 2) % 2), fsdp)
    near = j + 1 - 2 * (j % 2)
    far_mid = 2 - high
    far_outer = 3 - 3 * high
    arrival = (j, near, far_mid, far_outer)
    order = (far_outer, far_mid, near, j)

    def remote(src, dst, ssem, rsem, device):
        return pltpu.make_async_remote_copy(
            src_ref=src, dst_ref=dst, send_sem=ssem, recv_sem=rsem,
            device_id=device, device_id_type=MESH,
        )

    barrier = pltpu.get_barrier_semaphore()

    def greet(device):
        pl.semaphore_signal(barrier, inc=1, device_id=device, device_id_type=MESH)

    for d in range(1, NX):
        greet(along_x(d))
    greet(inward)

    @pl.when(mid)
    def _():
        greet(outward)

    greet(other_core)
    greet(other_half)
    for d in range(1, NZ):
        greet(along_z(d))

    own_rows = pl.ds(pl.multiple_of(i * TOK, TOK), TOK)
    half_rows = lambda h: pl.ds(pl.multiple_of(h * TOK, TOK), TOK)
    slice_rows = lambda s: pl.ds(pl.multiple_of(s * SLICE, SLICE), SLICE)

    loads = [
        pltpu.make_async_copy(hidden, h_v, local_sem.at[0]),
        pltpu.make_async_copy(value_grad, vg_buf.at[own_rows], local_sem.at[1]),
        pltpu.make_async_copy(weight, w_buf.at[j], local_sem.at[2]),
        pltpu.make_async_copy(delta.at[half_rows(core)], d_own, local_sem.at[3]),
        pltpu.make_async_copy(momentum, mom_v, local_sem.at[4]),
    ]
    for load in loads:
        load.start()

    pl.semaphore_wait(barrier, 13 + is_mid)

    vg_copies = [
        remote(value_grad, vg_buf.at[own_rows], x_send.at[d], x_recv.at[d], along_x(d))
        for d in range(1, NX)
    ]
    for copy in vg_copies:
        copy.start()
    w_first = remote(weight, w_buf.at[j], w_ssem.at[0], w_rsem.at[j], inward)
    w_second = remote(weight, w_buf.at[j], w_ssem.at[1], w_rsem.at[j], outward)
    w_first.start()

    @pl.when(mid)
    def _():
        w_second.start()

    core_half = remote(
        delta.at[half_rows(1 - core)], d_recv, c_ssem.at[0], c_rsem.at[0], other_core
    )
    core_half.start()

    loads[0].wait()

    def columns(f):
        return pl.ds(pl.multiple_of(f * ROWS, ROWS), ROWS)

    def add_square(f, total):
        block = h_v[:, columns(f)].astype(F32)
        return total + block * block

    squares = lax.fori_loop(0, 16, add_square, jnp.zeros((TOK, ROWS), F32))
    inv_v[...] = lax.rsqrt(jnp.sum(squares, axis=-1, keepdims=True) / D + EPSILON)

    @pl.loop(0, 16)
    def _(f):
        scaled = h_v[:, columns(f)].astype(F32) * inv_v[...]
        n_send[f] = (scaled * gain[:, columns(f)].astype(F32)).astype(BF16)

    n_copies = []
    for n, block in enumerate(order):
        for d in (1, 3, 2):
            copy = remote(
                n_send.at[((i + d) % NX) * NY + block], n_buf.at[block, own_rows],
                n_ssem.at[n, d], n_rsem.at[n, d], along_x(d),
            )
            copy.start()
            n_copies.append(copy)
    for block in range(NY):
        n_buf[block, own_rows] = n_send[i * NY + block]

    loads[3].wait()
    core_half.wait_recv()
    p_send[...] = (d_own[...].astype(F32) + d_recv[...].astype(F32)).astype(BF16)
    z_copies = [
        remote(
            p_send.at[slice_rows((z + d) % NZ)], z_recv.at[d - 1],
            z_ssem.at[d], z_rsem.at[d], along_z(d),
        )
        for d in range(1, NZ)
    ]
    for copy in z_copies:
        copy.start()

    def w_arrive(n):
        block = arrival[n]
        remote(
            w_buf.at[block], w_buf.at[block], w_ssem.at[0], w_rsem.at[block], inward
        ).wait_recv()

    def w_forward(n):
        block = arrival[n]
        return remote(
            w_buf.at[block], w_buf.at[block], w_ssem.at[n + 1], w_rsem.at[block],
            inward if n == 1 else outward,
        )

    def take_weight(n):
        w_arrive(n)

        @pl.when(mid)
        def _():
            w_forward(n).start()

    g_copies = []

    def send_grad(n):
        block = arrival[n]
        ng_send[n] = lax.dot_general(
            vg_buf[...], w_buf[block], (((1,), (1,)), ((), ())), preferred_element_type=F32
        ).astype(BF16)
        for d in (1, 3, 2):
            copy = remote(
                ng_send.at[n, pl.ds(pl.multiple_of(((i + d) % NX) * TOK, TOK), TOK)],
                ng_buf.at[i * NY + block], g_ssem.at[n, d], g_rsem.at[n, d], along_x(d),
            )
            copy.start()
            g_copies.append(copy)
        ng_buf[i * NY + block] = ng_send[n, own_rows]

    def make_weight_grad(n):
        for d in range(1, NX):
            n_copies[3 * n + (0, 0, 2, 1)[d]].wait_recv()
        block = order[n]
        wg_acc[block] = lax.dot_general(
            n_buf[block], vg_buf[...], (((0,), (0,)), ((), ())), preferred_element_type=F32
        ) * (1.0 / TOK)

    def first_hop(n):
        return remote(
            wg_send.at[order[n]], wg_recv.at[n], r_ssem.at[n], r_rsem.at[n], inward
        )

    def start_chain(n):
        @pl.when(outer)
        def _():
            wg_send[order[n]] = wg_acc[order[n]].astype(BF16)
            first_hop(n).start()

    def next_hop(slot):
        block, target, device = (
            (far_outer, 3, inward), (far_mid, 4, inward), None, (near, 3, outward),
        )[slot]
        return block, remote(
            wg_send.at[block], wg_recv.at[target], r_ssem.at[slot], r_rsem.at[target], device
        )

    def r_arrive(slot):
        remote(
            wg_recv.at[slot], wg_recv.at[slot], r_ssem.at[0], r_rsem.at[slot], inward
        ).wait_recv()

    def pass_on(slot):
        @pl.when(mid)
        def _():
            block, copy = next_hop(slot)
            r_arrive(slot)
            wg_send[block] = (wg_acc[block] + wg_recv[slot].astype(F32)).astype(BF16)
            copy.start()

    loads[1].wait()
    loads[2].wait()
    for copy in vg_copies:
        copy.wait_recv()
    send_grad(0)
    take_weight(1)

    for copy in z_copies:
        copy.wait_recv()
    total = (
        d_own[slice_rows(z)].astype(F32) + d_recv[slice_rows(z)].astype(F32)
    )
    for d in range(NZ - 1):
        total = total + z_recv[d].astype(F32)
    s_own[...] = total
    half_copy = remote(s_own, s_recv, c_ssem.at[1], c_rsem.at[1], other_half)
    half_copy.start()

    make_weight_grad(0)
    start_chain(0)
    send_grad(1)
    take_weight(2)
    make_weight_grad(1)
    start_chain(1)
    send_grad(2)

    half_copy.wait_recv()
    half_copy.wait_send()
    avg[core, slice_rows(z)] = (s_own[...] + s_recv[...]) / 32.0
    a_copies = [
        remote(
            avg.at[core, slice_rows(z)], avg.at[core, slice_rows(z)],
            a_ssem.at[d], a_rsem.at[d], along_z(d),
        )
        for d in range(1, NZ)
    ]
    for copy in a_copies:
        copy.start()

    make_weight_grad(2)
    start_chain(2)
    pass_on(0)
    take_weight(3)
    send_grad(3)
    make_weight_grad(3)

    v_acc = jnp.dot(n_buf[0], w_buf[0], preferred_element_type=F32)
    for block in range(1, NY):
        v_acc = v_acc + jnp.dot(n_buf[block], w_buf[block], preferred_element_type=F32)
    v_send[...] = v_acc.astype(BF16)
    v_copies = []
    for d in (1, 3, 2):
        copy = remote(
            v_send.at[pl.ds(pl.multiple_of(((i + d) % NX) * TOK, TOK), TOK)],
            v_recv.at[d - 1], v_ssem.at[d], v_rsem.at[d], along_x(d),
        )
        copy.start()
        v_copies.append(copy)

    for copy in a_copies:
        copy.wait_recv()
    core_full = remote(avg.at[core], avg.at[core], c_ssem.at[2], c_rsem.at[2], other_core)
    core_full.start()

    pass_on(3)
    pass_on(1)

    core_back = remote(
        avg.at[1 - core], avg.at[1 - core], c_ssem.at[2], c_rsem.at[2], other_core
    )
    core_back.wait_recv()
    loads[4].wait()
    for h in range(2):
        rows = pl.ds(h * TOK, TOK)
        new_momentum = MOMENT * mom_v[rows] + avg[h]
        nm_out[rows] = new_momentum
        os_out[rows] = -OUTER_RATE * (avg[h] + MOMENT * new_momentum)

    def gated_scaled(f):
        scaled = h_v[:, columns(f)].astype(F32) * inv_v[...]
        gated = ng_buf[f].astype(F32) * gain[:, columns(f)].astype(F32)
        return gated, scaled

    row_v[...] = jnp.zeros_like(row_v)

    def add_rows(f):
        gated, scaled = gated_scaled(f)
        row_v[...] += gated * scaled

    for n in range(NY):
        add_rows(i * NY + arrival[n])
    for n in range(NY):
        for d in range(1, NX):
            g_copies[3 * n + (0, 0, 2, 1)[d]].wait_recv()
            add_rows(((i + NX - d) % NX) * NY + arrival[n])
    mean = jnp.sum(row_v[...], axis=-1, keepdims=True) / D

    @pl.loop(0, 16)
    def _(f):
        gated, scaled = gated_scaled(f)
        hg_out[:, columns(f)] = (inv_v[...] * (gated - scaled * mean)).astype(BF16)

    @pl.when(outer)
    def _():
        r_arrive(3)
        wg_out[...] = (wg_acc[j] + wg_recv[3].astype(F32)).astype(BF16)

    @pl.when(mid)
    def _():
        r_arrive(2)
        r_arrive(4)
        wg_out[...] = (
            wg_acc[j] + wg_recv[2].astype(F32) + wg_recv[4].astype(F32)
        ).astype(BF16)

    value_sum = v_send[own_rows].astype(F32)
    for copy in v_copies:
        copy.wait_recv()
    for d in range(NX - 1):
        value_sum = value_sum + v_recv[d].astype(F32)
    val_out[...] = value_sum.astype(BF16)

    for copy in (*vg_copies, w_first, core_half, *n_copies, *z_copies, *g_copies, *a_copies):
        copy.wait_send()
    for copy in (*v_copies, core_full):
        copy.wait_send()

    @pl.when(mid)
    def _():
        w_second.wait_send()
        for n in range(1, NY):
            w_forward(n).wait_send()
        for slot in (0, 1, 3):
            next_hop(slot)[1].wait_send()

    @pl.when(outer)
    def _():
        for n in range(3):
            first_hop(n).wait_send()


def per_device(hidden, gain, value_grad, value_weight, outer_delta, momentum):
    anywhere = pl.BlockSpec(memory_space=pl.ANY)
    vmem = pl.BlockSpec(memory_space=pltpu.VMEM)
    dma = pltpu.SemaphoreType.DMA
    outs = pl.pallas_call(
        exchange,
        out_shape=(
            jax.ShapeDtypeStruct((TOK, D), BF16),
            jax.ShapeDtypeStruct((TOK, KV), BF16),
            jax.ShapeDtypeStruct((ROWS, KV), BF16),
            jax.ShapeDtypeStruct((ROWS, KV), F32),
            jax.ShapeDtypeStruct((ROWS, KV), F32),
        ),
        in_specs=[anywhere, vmem, anywhere, anywhere, anywhere, anywhere],
        out_specs=[vmem] * 5,
        scratch_shapes=[
            pltpu.VMEM((TOK, D), BF16),
            pltpu.VMEM((TOK, 1), F32),
            pltpu.VMEM((TOK, ROWS), F32),
            pltpu.VMEM((16, TOK, ROWS), BF16),
            pltpu.VMEM((NY, GROUP, ROWS), BF16),
            pltpu.VMEM((GROUP, KV), BF16),
            pltpu.VMEM((NY, ROWS, KV), BF16),
            pltpu.VMEM((NY, GROUP, ROWS), BF16),
            pltpu.VMEM((16, TOK, ROWS), BF16),
            pltpu.VMEM((GROUP, KV), BF16),
            pltpu.VMEM((NX - 1, TOK, KV), BF16),
            pltpu.VMEM((NY, ROWS, KV), F32),
            pltpu.VMEM((NY, ROWS, KV), BF16),
            pltpu.VMEM((5, ROWS, KV), BF16),
            pltpu.VMEM((TOK, KV), BF16),
            pltpu.VMEM((TOK, KV), BF16),
            pltpu.VMEM((TOK, KV), BF16),
            pltpu.VMEM((NZ - 1, SLICE, KV), BF16),
            pltpu.VMEM((SLICE, KV), F32),
            pltpu.VMEM((SLICE, KV), F32),
            pltpu.VMEM((2, TOK, KV), F32),
            pltpu.VMEM((ROWS, KV), F32),
            dma((5,)),
            dma((NX,)), dma((NX,)),
            dma((NY, NX)), dma((NY, NX)),
            dma((NY, NX)), dma((NY, NX)),
            dma((NX,)), dma((NX,)),
            dma((5,)), dma((NY,)),
            dma((5,)), dma((5,)),
            dma((3,)), dma((3,)),
            dma((NZ,)), dma((NZ,)),
            dma((NZ,)), dma((NZ,)),
        ],
        compiler_params=pltpu.CompilerParams(
            collective_id=0, has_side_effects=True, vmem_limit_bytes=40 * 1024 * 1024
        ),
    )(hidden[0], gain, value_grad[0], value_weight[0], outer_delta[0], momentum)
    hidden_grad, values, weight_grad, new_momentum, outer_step = outs
    return (values[None], weight_grad[None], hidden_grad[None], new_momentum, outer_step)


def solution(mesh):
    in_specs = (
        P("rep", "fsdp", None),
        P("rep", None),
        P("rep", "fsdp", None),
        P("rep", "fsdp", None),
        P("rep", "fsdp", None),
        P("fsdp", None),
    )
    out_specs = (
        P("rep", "fsdp", None),
        P("rep", "fsdp", None),
        P("rep", "fsdp", None),
        P("fsdp", None),
        P("fsdp", None),
    )
    return jax.shard_map(
        per_device, mesh=mesh, in_specs=in_specs, out_specs=out_specs, check_vma=False
    )
```

time: 429 us -> 59.1 us (0.14)
  the two profiles are of different devices: /device:TPU:1 before, /device:TPU:32 now
where the time goes in v1:
time: 59.1 us; the launch traced here: 58.8 us
  Pallas kernels  48.4 us (82%)
  local copies, waits for them, and re-layouts  9.69 us (16%)
  between operations  0.66 us (1%)
    pallas_call x1, Pallas kernels, per_device(): pl.pallas_call(exchange, out_shape=(jax.ShapeDtypeStruct((TOK, D), BF16),...  48.4 us
    unnamed x17, local copies, waits for them, and re-layouts  9.69 us

profile of v1, /device:TPU:32, one launch (start us, length us, event | category | flops | bytes accessed | tf_op | source)
XLA Modules:
  0.0 58.8 jit_solution(10524443303940978635)
XLA Ops:
  0.6 0.0 copy-start
  0.6 1.2 %copy-done = bf16[1,128,4096]{2,1,0:T(8,128)(2,1)S(1)} copy-done((bf16[1,128,4096]{2,1,0:T(8,128)(2,1)S(1)}, bf16[1,128,4096]{2,1,0:T(8,128)(2,1)}, u32[]{:S(2)}) %copy-start) | copy-done | bytes 1048600
  1.9 0.0 copy-start.1
  1.9 1.0 %copy-done.1 = f32[256,512]{1,0:T(8,128)S(1)} copy-done((f32[256,512]{1,0:T(8,128)S(1)}, f32[256,512]{1,0:T(8,128)}, u32[]{:S(2)}) %copy-start.1) | copy-done | bytes 524312
  2.9 0.0 copy-start.2
  2.9 0.9 %copy-done.2 = bf16[1,256,512]{2,1,0:T(8,128)(2,1)S(1)} copy-done((bf16[1,256,512]{2,1,0:T(8,128)(2,1)S(1)}, bf16[1,256,512]{2,1,0:T(8,128)(2,1)}, u32[]{:S(2)}) %copy-start.2) | copy-done | bytes 262168
  3.9 0.0 copy-start.3
  3.9 0.9 %copy-done.3 = bf16[1,256,512]{2,1,0:T(8,128)(2,1)S(1)} copy-done((bf16[1,256,512]{2,1,0:T(8,128)(2,1)S(1)}, bf16[1,256,512]{2,1,0:T(8,128)(2,1)}, u32[]{:S(2)}) %copy-start.3) | copy-done | bytes 262168
  4.8 0.0 copy-start.4
  4.8 0.9 %copy-done.4 = bf16[1,128,512]{2,1,0:T(8,128)(2,1)S(1)} copy-done((bf16[1,128,512]{2,1,0:T(8,128)(2,1)S(1)}, bf16[1,128,512]{2,1,0:T(8,128)(2,1)}, u32[]{:S(2)}) %copy-start.4) | copy-done | bytes 131096
  5.7 0.0 copy-start.5
  5.7 0.7 %copy-done.5 = bf16[1,4096]{1,0:T(2,128)(2,1)S(1)} copy-done((bf16[1,4096]{1,0:T(2,128)(2,1)S(1)}, bf16[1,4096]{1,0:T(2,128)(2,1)}, u32[]{:S(2)}) %copy-start.5) | copy-done | bytes 8216
  6.4 48.4 %shard_map.101 = (bf16[128,4096]{1,0:T(8,128)(2,1)S(1)}, bf16[128,512]{1,0:T(8,128)(2,1)S(1)}, bf16[256,512]{1,0:T(8,128)(2,1)S(1)}, f32[256,512]{1,0:T(8,128)S(1)}, f32[256,512]{1,0:T(8,128)S(1)}) custom-call(bf16[128,4096]{1,0:T(8,128)(2,1)S(1)} %bitcast.7, bf16[1,4096]{1,0:T(2,128)(2,1)S(1)} %copy-done.5, bf16[128,512]{1,0:T(8,128)(2,1)S(1)} %bitcast.12, ...), custom_call_target="tpu_custom_call" | custom-call | tf_op jit(solution)/shard_map/pallas_call | solution.py:383
  54.9 0.7 %copy.16 = bf16[1,128,512]{2,1,0:T(8,128)(2,1)} copy(bf16[1,128,512]{2,1,0:T(8,128)(2,1)S(1)} %bitcast.13) | data formatting | bytes 262144
  55.5 0.7 %copy.17 = bf16[1,256,512]{2,1,0:T(8,128)(2,1)} copy(bf16[1,256,512]{2,1,0:T(8,128)(2,1)S(1)} %bitcast.11) | data formatting | bytes 524288
  56.2 1.0 %copy.18 = bf16[1,128,4096]{2,1,0:T(8,128)(2,1)} copy(bf16[1,128,4096]{2,1,0:T(8,128)(2,1)S(1)} %bitcast.8) | data formatting | bytes 2097152
  57.2 0.8 %copy.19 = f32[256,512]{1,0:T(8,128)} copy(f32[256,512]{1,0:T(8,128)S(1)} %get-tuple-element.23) | data formatting | bytes 1048576
  58.0 0.8 %copy.20 = f32[256,512]{1,0:T(8,128)} copy(f32[256,512]{1,0:T(8,128)S(1)} %get-tuple-element.24) | data formatting | bytes 1048576
Async XLA Ops:
  0.6 1.2 %copy-start = (bf16[1,128,4096]{2,1,0:T(8,128)(2,1)S(1)}, bf16[1,128,4096]{2,1,0:T(8,128)(2,1)}, u32[]{:S(2)}) copy-start(bf16[1,128,4096]{2,1,0:T(8,128)(2,1)} %param.6) | copy-start | bytes 3145732
  1.9 1.0 %copy-start.1 = (f32[256,512]{1,0:T(8,128)S(1)}, f32[256,512]{1,0:T(8,128)}, u32[]{:S(2)}) copy-start(f32[256,512]{1,0:T(8,128)} %momentum.1) | copy-start | bytes 1572868
  2.9 0.9 %copy-start.2 = (bf16[1,256,512]{2,1,0:T(8,128)(2,1)S(1)}, bf16[1,256,512]{2,1,0:T(8,128)(2,1)}, u32[]{:S(2)}) copy-start(bf16[1,256,512]{2,1,0:T(8,128)(2,1)} %param.9) | copy-start | bytes 786436
  3.9 0.9 %copy-start.3 = (bf16[1,256,512]{2,1,0:T(8,128)(2,1)S(1)}, bf16[1,256,512]{2,1,0:T(8,128)(2,1)}, u32[]{:S(2)}) copy-start(bf16[1,256,512]{2,1,0:T(8,128)(2,1)} %param.10) | copy-start | bytes 786436
  4.8 0.9 %copy-start.4 = (bf16[1,128,512]{2,1,0:T(8,128)(2,1)S(1)}, bf16[1,128,512]{2,1,0:T(8,128)(2,1)}, u32[]{:S(2)}) copy-start(bf16[1,128,512]{2,1,0:T(8,128)(2,1)} %param.8) | copy-start | bytes 393220
  5.7 0.7 %copy-start.5 = (bf16[1,4096]{1,0:T(2,128)(2,1)S(1)}, bf16[1,4096]{1,0:T(2,128)(2,1)}, u32[]{:S(2)}) copy-start(bf16[1,4096]{1,0:T(2,128)(2,1)} %gain.1) | copy-start | bytes 24580

commit v2 on v1

--- a/solution.py
+++ b/solution.py
@@ -376,19 +376,31 @@
             first_hop(n).wait_send()
 
 
+def store(*refs):
+    sems = refs[-1]
+    copies = [
+        pltpu.make_async_copy(refs[k], refs[5 + k], sems.at[k]) for k in range(5)
+    ]
+    for copy in copies:
+        copy.start()
+    for copy in copies:
+        copy.wait()
+
+
 def per_device(hidden, gain, value_grad, value_weight, outer_delta, momentum):
     anywhere = pl.BlockSpec(memory_space=pl.ANY)
     vmem = pl.BlockSpec(memory_space=pltpu.VMEM)
     dma = pltpu.SemaphoreType.DMA
+    shapes = (
+        jax.ShapeDtypeStruct((TOK, D), BF16),
+        jax.ShapeDtypeStruct((TOK, KV), BF16),
+        jax.ShapeDtypeStruct((ROWS, KV), BF16),
+        jax.ShapeDtypeStruct((ROWS, KV), F32),
+        jax.ShapeDtypeStruct((ROWS, KV), F32),
+    )
     outs = pl.pallas_call(
         exchange,
-        out_shape=(
-            jax.ShapeDtypeStruct((TOK, D), BF16),
-            jax.ShapeDtypeStruct((TOK, KV), BF16),
-            jax.ShapeDtypeStruct((ROWS, KV), BF16),
-            jax.ShapeDtypeStruct((ROWS, KV), F32),
-            jax.ShapeDtypeStruct((ROWS, KV), F32),
-        ),
+        out_shape=shapes,
         in_specs=[anywhere, vmem, anywhere, anywhere, anywhere, anywhere],
         out_specs=[vmem] * 5,
         scratch_shapes=[
@@ -428,8 +440,15 @@
         compiler_params=pltpu.CompilerParams(
             collective_id=0, has_side_effects=True, vmem_limit_bytes=40 * 1024 * 1024
         ),
-    )(hidden[0], gain, value_grad[0], value_weight[0], outer_delta[0], momentum)
-    hidden_grad, values, weight_grad, new_momentum, outer_step = outs
+    )(*[pltpu.with_memory_space_constraint(a, pltpu.HBM) for a in (hidden[0], gain, value_grad[0], value_weight[0], outer_delta[0], momentum)])
+    hidden_grad, values, weight_grad, new_momentum, outer_step = pl.pallas_call(
+        store,
+        out_shape=shapes,
+        in_specs=[anywhere] * 5,
+        out_specs=[anywhere] * 5,
+        scratch_shapes=[dma((5,))],
+        compiler_params=pltpu.CompilerParams(vmem_limit_bytes=1024 * 1024),
+    )(*outs)
     return (values[None], weight_grad[None], hidden_grad[None], new_momentum, outer_step)
 
 

time: 59.1 us -> 51.6 us (0.87)
  local copies, waits for them, and re-layouts: 9.69 us -> 0 us
  Pallas kernels: 48.4 us -> 50.7 us
    unnamed x17 -> x0, local copies, waits for them, and re-layouts: 9.69 us -> none
    pallas_call x1 -> x2, Pallas kernels: 48.4 us -> 50.7 us  [the longest x1 49.2 us: per_device(): pl.pallas_call(exchange, out_shape=shapes, in_specs=[anywhere, vmem, anyw...]
where the time goes in v2:
time: 51.6 us; the launch traced here: 51.4 us
  Pallas kernels  50.7 us (98%)
  between operations  0.64 us (1%)
    pallas_call x1, Pallas kernels, per_device(): pl.pallas_call(exchange, out_shape=shapes, in_specs=[anywhere, vmem, anyw...  49.2 us
    pallas_call x1, Pallas kernels, per_device(): pl.pallas_call(store, out_shape=shapes, in_specs=[anywhere] * 5, out_spec...  1.49 us

profile of v2, /device:TPU:32, one launch (start us, length us, event | category | flops | bytes accessed | tf_op | source)
XLA Modules:
  0.0 51.4 jit_solution(3263320028272901107)
XLA Ops:
  0.6 49.2 %shard_map.101 = (bf16[128,4096]{1,0:T(8,128)(2,1)S(1)}, bf16[128,512]{1,0:T(8,128)(2,1)S(1)}, bf16[256,512]{1,0:T(8,128)(2,1)S(1)}, f32[256,512]{1,0:T(8,128)S(1)}, f32[256,512]{1,0:T(8,128)S(1)}) custom-call(bf16[128,4096]{1,0:T(8,128)(2,1)} %bitcast.7, bf16[1,4096]{1,0:T(2,128)(2,1)} %gain.1, bf16[128,512]{1,0:T(8,128)(2,1)} %bitcast.10, ...), custom_call_target="tpu_custom_call" | custom-call | tf_op jit(solution)/shard_map/pallas_call | solution.py:401
  49.9 1.5 %shard_map.102 = (bf16[128,4096]{1,0:T(8,128)(2,1)}, bf16[128,512]{1,0:T(8,128)(2,1)}, bf16[256,512]{1,0:T(8,128)(2,1)}, f32[256,512]{1,0:T(8,128)}, f32[256,512]{1,0:T(8,128)}) custom-call(bf16[128,4096]{1,0:T(8,128)(2,1)S(1)} %get-tuple-element.15.refs_0_, bf16[128,512]{1,0:T(8,128)(2,1)S(1)} %get-tuple-element.16.refs_1_, ...), custom_call_target="tpu_custom_call" | custom-call | tf_op jit(solution)/shard_map/pallas_call | solution.py:444

commit v3 on v2

--- a/solution.py
+++ b/solution.py
@@ -29,9 +29,10 @@
     hg_out, val_out, wg_out, nm_out, os_out,
     h_v, inv_v, row_v, n_send, n_buf, vg_buf, w_buf, ng_send, ng_buf,
     v_send, v_recv, wg_acc, wg_send, wg_recv,
-    d_own, d_recv, p_send, z_recv, s_own, s_recv, avg, mom_v,
+    d_own, d_recv, q_send, q_recv, p_send, z_recv, avg, mom_v,
     local_sem, x_send, x_recv, n_ssem, n_rsem, g_ssem, g_rsem, v_ssem, v_rsem,
     w_ssem, w_rsem, r_ssem, r_rsem, c_ssem, c_rsem, z_ssem, z_rsem, a_ssem, a_rsem,
+    below_sem, above_sem,
 ):
     rep = lax.axis_index("rep")
     fsdp = lax.axis_index("fsdp")
@@ -79,8 +80,14 @@
 
     greet(other_core)
     greet(other_half)
-    for d in range(1, NZ):
-        greet(along_z(d))
+
+    @pl.when(z > 0)
+    def _():
+        greet(along_z(NZ - 1))
+
+    @pl.when(z < NZ - 1)
+    def _():
+        greet(along_z(1))
 
     own_rows = pl.ds(pl.multiple_of(i * TOK, TOK), TOK)
     half_rows = lambda h: pl.ds(pl.multiple_of(h * TOK, TOK), TOK)
@@ -96,7 +103,8 @@
     for load in loads:
         load.start()
 
-    pl.semaphore_wait(barrier, 13 + is_mid)
+    z_ends = (NZ - 1 - z) // (NZ - 1) + z // (NZ - 1)
+    pl.semaphore_wait(barrier, 8 + is_mid - z_ends)
 
     vg_copies = [
         remote(value_grad, vg_buf.at[own_rows], x_send.at[d], x_recv.at[d], along_x(d))
@@ -104,13 +112,21 @@
     ]
     for copy in vg_copies:
         copy.start()
-    w_first = remote(weight, w_buf.at[j], w_ssem.at[0], w_rsem.at[j], inward)
-    w_second = remote(weight, w_buf.at[j], w_ssem.at[1], w_rsem.at[j], outward)
-    w_first.start()
-
-    @pl.when(mid)
-    def _():
-        w_second.start()
+    def w_half(h):
+        return pl.ds(h * (ROWS // 2), ROWS // 2)
+
+    def w_own(h, way, device):
+        return remote(
+            weight.at[w_half(h)], w_buf.at[j, w_half(h)],
+            w_ssem.at[way, h], w_rsem.at[j, h], device,
+        )
+
+    for h in range(2):
+        w_own(h, 0, inward).start()
+
+        @pl.when(mid)
+        def _():
+            w_own(h, 1, outward).start()
 
     core_half = remote(
         delta.at[half_rows(1 - core)], d_recv, c_ssem.at[0], c_rsem.at[0], other_core
@@ -146,9 +162,29 @@
     for block in range(NY):
         n_buf[block, own_rows] = n_send[i * NY + block]
 
+    @pl.when(z > 0)
+    def _():
+        pl.semaphore_wait(below_sem, 1)
+
+    @pl.when(z < NZ - 1)
+    def _():
+        pl.semaphore_signal(
+            below_sem, inc=1, device_id=along_z(1), device_id_type=MESH
+        )
+
+    for d in range(2, NZ):
+        @pl.when(z >= d)
+        def _():
+            pl.semaphore_signal(
+                above_sem, inc=1, device_id=along_z(NZ - d), device_id_type=MESH
+            )
+
     loads[3].wait()
     core_half.wait_recv()
-    p_send[...] = (d_own[...].astype(F32) + d_recv[...].astype(F32)).astype(BF16)
+    q_send[...] = (d_own[...].astype(F32) + d_recv[...].astype(F32)).astype(BF16)
+    half_copy = remote(q_send, q_recv, c_ssem.at[1], c_rsem.at[1], other_half)
+    half_copy.start()
+
     z_copies = [
         remote(
             p_send.at[slice_rows((z + d) % NZ)], z_recv.at[d - 1],
@@ -156,28 +192,66 @@
         )
         for d in range(1, NZ)
     ]
-    for copy in z_copies:
-        copy.start()
-
-    def w_arrive(n):
-        block = arrival[n]
+
+    late = z >= NZ // 2
+
+    def send_slices():
+        half_copy.wait_recv()
+        p_send[...] = (q_send[...].astype(F32) + q_recv[...].astype(F32)).astype(BF16)
+
+        @pl.when(z < NZ - 2)
+        def _():
+            pl.semaphore_wait(above_sem, NZ - 2 - z)
+
+        for copy in z_copies:
+            copy.start()
+
+    a_copies = [
         remote(
-            w_buf.at[block], w_buf.at[block], w_ssem.at[0], w_rsem.at[block], inward
-        ).wait_recv()
-
-    def w_forward(n):
-        block = arrival[n]
+            avg.at[core, slice_rows(z)], avg.at[core, slice_rows(z)],
+            a_ssem.at[d], a_rsem.at[d], along_z(d),
+        )
+        for d in range(1, NZ)
+    ]
+
+    def send_average():
+        for copy in z_copies:
+            copy.wait_recv()
+        total = q_send[slice_rows(z)].astype(F32) + q_recv[slice_rows(z)].astype(F32)
+        for d in range(NZ - 1):
+            total = total + z_recv[d].astype(F32)
+        avg[core, slice_rows(z)] = total / 32.0
+        for copy in a_copies:
+            copy.start()
+
+    core_full = remote(avg.at[core], avg.at[core], c_ssem.at[2], c_rsem.at[2], other_core)
+    core_back = remote(
+        avg.at[1 - core], avg.at[1 - core], c_ssem.at[2], c_rsem.at[2], other_core
+    )
+
+    def share_average():
+        for copy in a_copies:
+            copy.wait_recv()
+        core_full.start()
+
+    def w_forward(n, h):
+        part = w_buf.at[arrival[n], w_half(h)]
         return remote(
-            w_buf.at[block], w_buf.at[block], w_ssem.at[n + 1], w_rsem.at[block],
+            part, part, w_ssem.at[n + 1, h], w_rsem.at[arrival[n], h],
             inward if n == 1 else outward,
         )
 
-    def take_weight(n):
-        w_arrive(n)
-
+    def forward_weight(n, h):
         @pl.when(mid)
         def _():
-            w_forward(n).start()
+            w_forward(n, h).wait_recv()
+            w_forward(n, h).start()
+
+    def await_weight(n):
+        @pl.when(outer)
+        def _():
+            for h in range(2):
+                w_forward(n, h).wait_recv()
 
     g_copies = []
 
@@ -235,51 +309,34 @@
             wg_send[block] = (wg_acc[block] + wg_recv[slot].astype(F32)).astype(BF16)
             copy.start()
 
+    for h in range(2):
+        forward_weight(1, h)
+        forward_weight(2, h)
     loads[1].wait()
     loads[2].wait()
     for copy in vg_copies:
         copy.wait_recv()
     send_grad(0)
-    take_weight(1)
-
-    for copy in z_copies:
-        copy.wait_recv()
-    total = (
-        d_own[slice_rows(z)].astype(F32) + d_recv[slice_rows(z)].astype(F32)
-    )
-    for d in range(NZ - 1):
-        total = total + z_recv[d].astype(F32)
-    s_own[...] = total
-    half_copy = remote(s_own, s_recv, c_ssem.at[1], c_rsem.at[1], other_half)
-    half_copy.start()
-
+    pl.when(late)(send_slices)
+    forward_weight(3, 0)
+    await_weight(1)
+    send_grad(1)
     make_weight_grad(0)
     start_chain(0)
-    send_grad(1)
-    take_weight(2)
+    pl.when(jnp.logical_not(late))(send_slices)
+    forward_weight(3, 1)
     make_weight_grad(1)
     start_chain(1)
+    pl.when(late)(send_average)
+    await_weight(2)
     send_grad(2)
-
-    half_copy.wait_recv()
-    half_copy.wait_send()
-    avg[core, slice_rows(z)] = (s_own[...] + s_recv[...]) / 32.0
-    a_copies = [
-        remote(
-            avg.at[core, slice_rows(z)], avg.at[core, slice_rows(z)],
-            a_ssem.at[d], a_rsem.at[d], along_z(d),
-        )
-        for d in range(1, NZ)
-    ]
-    for copy in a_copies:
-        copy.start()
-
     make_weight_grad(2)
     start_chain(2)
     pass_on(0)
-    take_weight(3)
+    make_weight_grad(3)
+    pl.when(jnp.logical_not(late))(send_average)
+    await_weight(3)
     send_grad(3)
-    make_weight_grad(3)
 
     v_acc = jnp.dot(n_buf[0], w_buf[0], preferred_element_type=F32)
     for block in range(1, NY):
@@ -294,17 +351,50 @@
         copy.start()
         v_copies.append(copy)
 
-    for copy in a_copies:
-        copy.wait_recv()
-    core_full = remote(avg.at[core], avg.at[core], c_ssem.at[2], c_rsem.at[2], other_core)
-    core_full.start()
-
+    def gated_scaled(f):
+        scaled = h_v[:, columns(f)].astype(F32) * inv_v[...]
+        gated = ng_buf[f].astype(F32) * gain[:, columns(f)].astype(F32)
+        return gated, scaled
+
+    row_v[...] = jnp.zeros_like(row_v)
+
+    def add_rows(f):
+        gated, scaled = gated_scaled(f)
+        row_v[...] += gated * scaled
+
+    def take_grad(n):
+        add_rows(i * NY + arrival[n])
+        for d in range(1, NX):
+            g_copies[3 * n + (0, 0, 2, 1)[d]].wait_recv()
+            add_rows(((i + NX - d) % NX) * NY + arrival[n])
+
+    take_grad(0)
+    pass_on(1)
     pass_on(3)
-    pass_on(1)
-
-    core_back = remote(
-        avg.at[1 - core], avg.at[1 - core], c_ssem.at[2], c_rsem.at[2], other_core
-    )
+    take_grad(1)
+    share_average()
+    take_grad(2)
+    take_grad(3)
+    mean = jnp.sum(row_v[...], axis=-1, keepdims=True) / D
+
+    @pl.loop(0, 16)
+    def _(f):
+        gated, scaled = gated_scaled(f)
+        hg_out[:, columns(f)] = (inv_v[...] * (gated - scaled * mean)).astype(BF16)
+
+    @pl.when(outer)
+    def _():
+        r_arrive(3)
+        wg_out[...] = (wg_acc[j] + wg_recv[3].astype(F32)).astype(BF16)
+
+    @pl.when(mid)
+    def _():
+        r_arrive(2)
+        r_arrive(4)
+        wg_out[...] = (
+            wg_acc[j] + wg_recv[2].astype(F32) + wg_recv[4].astype(F32)
+        ).astype(BF16)
+
     core_back.wait_recv()
     loads[4].wait()
     for h in range(2):
@@ -313,43 +403,6 @@
         nm_out[rows] = new_momentum
         os_out[rows] = -OUTER_RATE * (avg[h] + MOMENT * new_momentum)
 
-    def gated_scaled(f):
-        scaled = h_v[:, columns(f)].astype(F32) * inv_v[...]
-        gated = ng_buf[f].astype(F32) * gain[:, columns(f)].astype(F32)
-        return gated, scaled
-
-    row_v[...] = jnp.zeros_like(row_v)
-
-    def add_rows(f):
-        gated, scaled = gated_scaled(f)
-        row_v[...] += gated * scaled
-
-    for n in range(NY):
-        add_rows(i * NY + arrival[n])
-    for n in range(NY):
-        for d in range(1, NX):
-            g_copies[3 * n + (0, 0, 2, 1)[d]].wait_recv()
-            add_rows(((i + NX - d) % NX) * NY + arrival[n])
-    mean = jnp.sum(row_v[...], axis=-1, keepdims=True) / D
-
-    @pl.loop(0, 16)
-    def _(f):
-        gated, scaled = gated_scaled(f)
-        hg_out[:, columns(f)] = (inv_v[...] * (gated - scaled * mean)).astype(BF16)
-
-    @pl.when(outer)
-    def _():
-        r_arrive(3)
-        wg_out[...] = (wg_acc[j] + wg_recv[3].astype(F32)).astype(BF16)
-
-    @pl.when(mid)
-    def _():
-        r_arrive(2)
-        r_arrive(4)
-        wg_out[...] = (
-            wg_acc[j] + wg_recv[2].astype(F32) + wg_recv[4].astype(F32)
-        ).astype(BF16)
-
     value_sum = v_send[own_rows].astype(F32)
     for copy in v_copies:
         copy.wait_recv()
@@ -357,16 +410,17 @@
         value_sum = value_sum + v_recv[d].astype(F32)
     val_out[...] = value_sum.astype(BF16)
 
-    for copy in (*vg_copies, w_first, core_half, *n_copies, *z_copies, *g_copies, *a_copies):
+    for copy in (*vg_copies, w_own(0, 0, inward), w_own(1, 0, inward), core_half, *n_copies, *z_copies, *g_copies, *a_copies):
         copy.wait_send()
-    for copy in (*v_copies, core_full):
+    for copy in (*v_copies, core_full, half_copy):
         copy.wait_send()
 
     @pl.when(mid)
     def _():
-        w_second.wait_send()
-        for n in range(1, NY):
-            w_forward(n).wait_send()
+        for h in range(2):
+            w_own(h, 1, outward).wait_send()
+            for n in range(1, NY):
+                w_forward(n, h).wait_send()
         for slot in (0, 1, 3):
             next_hop(slot)[1].wait_send()
 
@@ -421,9 +475,9 @@
             pltpu.VMEM((TOK, KV), BF16),
             pltpu.VMEM((TOK, KV), BF16),
             pltpu.VMEM((TOK, KV), BF16),
+            pltpu.VMEM((TOK, KV), BF16),
+            pltpu.VMEM((TOK, KV), BF16),
             pltpu.VMEM((NZ - 1, SLICE, KV), BF16),
-            pltpu.VMEM((SLICE, KV), F32),
-            pltpu.VMEM((SLICE, KV), F32),
             pltpu.VMEM((2, TOK, KV), F32),
             pltpu.VMEM((ROWS, KV), F32),
             dma((5,)),
@@ -431,11 +485,13 @@
             dma((NY, NX)), dma((NY, NX)),
             dma((NY, NX)), dma((NY, NX)),
             dma((NX,)), dma((NX,)),
-            dma((5,)), dma((NY,)),
+            dma((5, 2)), dma((NY, 2)),
             dma((5,)), dma((5,)),
             dma((3,)), dma((3,)),
             dma((NZ,)), dma((NZ,)),
             dma((NZ,)), dma((NZ,)),
+            pltpu.SemaphoreType.REGULAR,
+            pltpu.SemaphoreType.REGULAR,
         ],
         compiler_params=pltpu.CompilerParams(
             collective_id=0, has_side_effects=True, vmem_limit_bytes=40 * 1024 * 1024

time: 51.6 us -> 48.4 us (0.938)
  the two profiles are of different devices: /device:TPU:32 before, /device:TPU:1 now
where the time goes in v3:
time: 48.4 us; the launch traced here: 48.1 us
  Pallas kernels  47.5 us (98%)
  between operations  0.64 us (1%)
    pallas_call x1, Pallas kernels, per_device(): pl.pallas_call(exchange, out_shape=shapes, in_specs=[anywhere, vmem, anyw...  46 us
    pallas_call x1, Pallas kernels, per_device(): pl.pallas_call(store, out_shape=shapes, in_specs=[anywhere] * 5, out_spec...  1.49 us

profile of v3, /device:TPU:1, one launch (start us, length us, event | category | flops | bytes accessed | tf_op | source)
XLA Modules:
  0.0 48.1 jit_solution(5709775183016717675)
XLA Ops:
  0.6 46.0 %shard_map.101 = (bf16[128,4096]{1,0:T(8,128)(2,1)S(1)}, bf16[128,512]{1,0:T(8,128)(2,1)S(1)}, bf16[256,512]{1,0:T(8,128)(2,1)S(1)}, f32[256,512]{1,0:T(8,128)S(1)}, f32[256,512]{1,0:T(8,128)S(1)}) custom-call(bf16[128,4096]{1,0:T(8,128)(2,1)} %bitcast.7, bf16[1,4096]{1,0:T(2,128)(2,1)} %gain.1, bf16[128,512]{1,0:T(8,128)(2,1)} %bitcast.10, ...), custom_call_target="tpu_custom_call" | custom-call | tf_op jit(solution)/shard_map/pallas_call | solution.py:455
  46.6 1.5 %shard_map.102 = (bf16[128,4096]{1,0:T(8,128)(2,1)}, bf16[128,512]{1,0:T(8,128)(2,1)}, bf16[256,512]{1,0:T(8,128)(2,1)}, f32[256,512]{1,0:T(8,128)}, f32[256,512]{1,0:T(8,128)}) custom-call(bf16[128,4096]{1,0:T(8,128)(2,1)S(1)} %get-tuple-element.15.refs_0_, bf16[128,512]{1,0:T(8,128)(2,1)S(1)} %get-tuple-element.16.refs_1_, ...), custom_call_target="tpu_custom_call" | custom-call | tf_op jit(solution)/shard_map/pallas_call | solution.py:500

commit v4 on v3

--- a/solution.py
+++ b/solution.py
@@ -28,7 +28,7 @@
     hidden, gain, value_grad, weight, delta, momentum,
     hg_out, val_out, wg_out, nm_out, os_out,
     h_v, inv_v, row_v, n_send, n_buf, vg_buf, w_buf, ng_send, ng_buf,
-    v_send, v_recv, wg_acc, wg_send, wg_recv,
+    v_part, v_send, v_mid, v_recv, wg_acc, wg_send, wg_recv,
     d_own, d_recv, q_send, q_recv, p_send, z_recv, avg, mom_v,
     local_sem, x_send, x_recv, n_ssem, n_rsem, g_ssem, g_rsem, v_ssem, v_rsem,
     w_ssem, w_rsem, r_ssem, r_rsem, c_ssem, c_rsem, z_ssem, z_rsem, a_ssem, a_rsem,
@@ -79,15 +79,17 @@
         greet(outward)
 
     greet(other_core)
+    late = z >= NZ // 2
+
     greet(other_half)
-
-    @pl.when(z > 0)
-    def _():
-        greet(along_z(NZ - 1))
-
-    @pl.when(z < NZ - 1)
-    def _():
-        greet(along_z(1))
+    for d in range(1, NZ):
+        there = (z + d) % NZ
+        both_late = jnp.logical_and(late, there >= NZ // 2)
+        beside = jnp.logical_or(there == z + 1, there == z - 1)
+
+        @pl.when(jnp.logical_or(both_late, beside))
+        def _():
+            greet(along_z(d))
 
     own_rows = pl.ds(pl.multiple_of(i * TOK, TOK), TOK)
     half_rows = lambda h: pl.ds(pl.multiple_of(h * TOK, TOK), TOK)
@@ -103,15 +105,29 @@
     for load in loads:
         load.start()
 
-    z_ends = (NZ - 1 - z) // (NZ - 1) + z // (NZ - 1)
-    pl.semaphore_wait(barrier, 8 + is_mid - z_ends)
-
-    vg_copies = [
+    upper = z // 4
+    first, fifth = 1 - (z + 7) // 8, upper * (1 - (z + 3) // 8)
+    z_greeted = (1 - upper) * (2 - first) + upper * (3 + fifth)
+    pl.semaphore_wait(barrier, 6 + is_mid + z_greeted)
+
+    vg_first = [
         remote(value_grad, vg_buf.at[own_rows], x_send.at[d], x_recv.at[d], along_x(d))
-        for d in range(1, NX)
+        for d in (1, 3)
     ]
-    for copy in vg_copies:
+    for copy in vg_first:
         copy.start()
+    half_tok = TOK // 2
+
+    def part_rows(d, h):
+        return pl.ds(pl.multiple_of(((i + d) % NX) * TOK + h * half_tok, half_tok), half_tok)
+
+    vg_second = [
+        remote(
+            vg_buf.at[part_rows(NX - d, h)], vg_buf.at[part_rows(NX - d, h)],
+            x_send.at[2 * h], x_recv.at[2 * h], along_x(d),
+        )
+        for d, h in ((1, 0), (3, 1))
+    ]
     def w_half(h):
         return pl.ds(h * (ROWS // 2), ROWS // 2)
 
@@ -133,6 +149,22 @@
     )
     core_half.start()
 
+    def tell(semaphore, device):
+        pl.semaphore_signal(semaphore, inc=1, device_id=device, device_id_type=MESH)
+
+    @pl.when(jnp.logical_and(z > 0, z <= 4))
+    def _():
+        pl.semaphore_wait(below_sem, 1)
+
+    @pl.when(z < 4)
+    def _():
+        tell(below_sem, along_z(1))
+
+    @pl.when(z == 4)
+    def _():
+        for d in range(1, 4):
+            tell(below_sem, along_z(d))
+
     loads[0].wait()
 
     def columns(f):
@@ -149,6 +181,15 @@
     def _(f):
         scaled = h_v[:, columns(f)].astype(F32) * inv_v[...]
         n_send[f] = (scaled * gain[:, columns(f)].astype(F32)).astype(BF16)
+
+    @pl.when(z > 4)
+    def _():
+        pl.semaphore_wait(below_sem, 1)
+
+    for d in range(2, NZ):
+        @pl.when(jnp.logical_and(z >= d, z < d + 4))
+        def _():
+            tell(above_sem, along_z(NZ - d))
 
     n_copies = []
     for n, block in enumerate(order):
@@ -159,25 +200,12 @@
             )
             copy.start()
             n_copies.append(copy)
+        if n == 0:
+            for first, second in zip(vg_first, vg_second):
+                first.wait_recv()
+                second.start()
     for block in range(NY):
         n_buf[block, own_rows] = n_send[i * NY + block]
-
-    @pl.when(z > 0)
-    def _():
-        pl.semaphore_wait(below_sem, 1)
-
-    @pl.when(z < NZ - 1)
-    def _():
-        pl.semaphore_signal(
-            below_sem, inc=1, device_id=along_z(1), device_id_type=MESH
-        )
-
-    for d in range(2, NZ):
-        @pl.when(z >= d)
-        def _():
-            pl.semaphore_signal(
-                above_sem, inc=1, device_id=along_z(NZ - d), device_id_type=MESH
-            )
 
     loads[3].wait()
     core_half.wait_recv()
@@ -193,15 +221,13 @@
         for d in range(1, NZ)
     ]
 
-    late = z >= NZ // 2
-
     def send_slices():
         half_copy.wait_recv()
         p_send[...] = (q_send[...].astype(F32) + q_recv[...].astype(F32)).astype(BF16)
 
-        @pl.when(z < NZ - 2)
-        def _():
-            pl.semaphore_wait(above_sem, NZ - 2 - z)
+        @pl.when(z < 4)
+        def _():
+            pl.semaphore_wait(above_sem, 6 - z)
 
         for copy in z_copies:
             copy.start()
@@ -220,7 +246,7 @@
         total = q_send[slice_rows(z)].astype(F32) + q_recv[slice_rows(z)].astype(F32)
         for d in range(NZ - 1):
             total = total + z_recv[d].astype(F32)
-        avg[core, slice_rows(z)] = total / 32.0
+        avg[core, slice_rows(z)] = (total / 32.0).astype(BF16)
         for copy in a_copies:
             copy.start()
 
@@ -314,42 +340,54 @@
         forward_weight(2, h)
     loads[1].wait()
     loads[2].wait()
-    for copy in vg_copies:
+    for copy in vg_second:
         copy.wait_recv()
     send_grad(0)
-    pl.when(late)(send_slices)
     forward_weight(3, 0)
     await_weight(1)
-    send_grad(1)
     make_weight_grad(0)
     start_chain(0)
-    pl.when(jnp.logical_not(late))(send_slices)
+    send_grad(1)
+    pl.when(late)(send_slices)
     forward_weight(3, 1)
     make_weight_grad(1)
     start_chain(1)
-    pl.when(late)(send_average)
+    pl.when(jnp.logical_not(late))(send_slices)
     await_weight(2)
     send_grad(2)
     make_weight_grad(2)
     start_chain(2)
     pass_on(0)
+    pl.when(late)(send_average)
     make_weight_grad(3)
-    pl.when(jnp.logical_not(late))(send_average)
     await_weight(3)
-    send_grad(3)
 
     v_acc = jnp.dot(n_buf[0], w_buf[0], preferred_element_type=F32)
     for block in range(1, NY):
         v_acc = v_acc + jnp.dot(n_buf[block], w_buf[block], preferred_element_type=F32)
-    v_send[...] = v_acc.astype(BF16)
+    v_part[...] = v_acc
     v_copies = []
-    for d in (1, 3, 2):
-        copy = remote(
-            v_send.at[pl.ds(pl.multiple_of(((i + d) % NX) * TOK, TOK), TOK)],
-            v_recv.at[d - 1], v_ssem.at[d], v_rsem.at[d], along_x(d),
-        )
+    for d, h in ((1, 0), (3, 1)):
+        rows = part_rows(2, h)
+        v_send[rows] = v_part[rows].astype(BF16)
+        copy = remote(v_send.at[rows], v_mid.at[h], v_ssem.at[h], v_rsem.at[h], along_x(d))
         copy.start()
         v_copies.append(copy)
+    send_grad(3)
+    pl.when(jnp.logical_not(late))(send_average)
+
+    def send_values():
+        for d, h in ((1, 0), (3, 1)):
+            v_copies[h].wait_recv()
+            added, kept = part_rows(d, h), part_rows(d, 1 - h)
+            v_send[added] = (v_part[added] + v_mid[h].astype(F32)).astype(BF16)
+            v_send[kept] = v_part[kept].astype(BF16)
+            rows = pl.ds(pl.multiple_of(((i + d) % NX) * TOK, TOK), TOK)
+            copy = remote(
+                v_send.at[rows], v_recv.at[h], v_ssem.at[2 + h], v_rsem.at[2 + h], along_x(d)
+            )
+            copy.start()
+            v_copies.append(copy)
 
     def gated_scaled(f):
         scaled = h_v[:, columns(f)].astype(F32) * inv_v[...]
@@ -368,12 +406,13 @@
             g_copies[3 * n + (0, 0, 2, 1)[d]].wait_recv()
             add_rows(((i + NX - d) % NX) * NY + arrival[n])
 
-    take_grad(0)
     pass_on(1)
     pass_on(3)
+    take_grad(0)
     take_grad(1)
+    take_grad(2)
+    send_values()
     share_average()
-    take_grad(2)
     take_grad(3)
     mean = jnp.sum(row_v[...], axis=-1, keepdims=True) / D
 
@@ -399,18 +438,18 @@
     loads[4].wait()
     for h in range(2):
         rows = pl.ds(h * TOK, TOK)
-        new_momentum = MOMENT * mom_v[rows] + avg[h]
+        average = avg[h].astype(F32)
+        new_momentum = MOMENT * mom_v[rows] + average
         nm_out[rows] = new_momentum
-        os_out[rows] = -OUTER_RATE * (avg[h] + MOMENT * new_momentum)
-
-    value_sum = v_send[own_rows].astype(F32)
-    for copy in v_copies:
-        copy.wait_recv()
-    for d in range(NX - 1):
-        value_sum = value_sum + v_recv[d].astype(F32)
+        os_out[rows] = -OUTER_RATE * (average + MOMENT * new_momentum)
+
+    value_sum = v_part[own_rows]
+    for h in range(2):
+        v_copies[2 + h].wait_recv()
+        value_sum = value_sum + v_recv[h].astype(F32)
     val_out[...] = value_sum.astype(BF16)
 
-    for copy in (*vg_copies, w_own(0, 0, inward), w_own(1, 0, inward), core_half, *n_copies, *z_copies, *g_copies, *a_copies):
+    for copy in (*vg_first, *vg_second, w_own(0, 0, inward), w_own(1, 0, inward), core_half, *n_copies, *z_copies, *g_copies, *a_copies):
         copy.wait_send()
     for copy in (*v_copies, core_full, half_copy):
         copy.wait_send()
@@ -467,8 +506,10 @@
             pltpu.VMEM((NY, ROWS, KV), BF16),
             pltpu.VMEM((NY, GROUP, ROWS), BF16),
             pltpu.VMEM((16, TOK, ROWS), BF16),
+            pltpu.VMEM((GROUP, KV), F32),
             pltpu.VMEM((GROUP, KV), BF16),
-            pltpu.VMEM((NX - 1, TOK, KV), BF16),
+            pltpu.VMEM((2, TOK // 2, KV), BF16),
+            pltpu.VMEM((2, TOK, KV), BF16),
             pltpu.VMEM((NY, ROWS, KV), F32),
             pltpu.VMEM((NY, ROWS, KV), BF16),
             pltpu.VMEM((5, ROWS, KV), BF16),
@@ -478,7 +519,7 @@
             pltpu.VMEM((TOK, KV), BF16),
             pltpu.VMEM((TOK, KV), BF16),
             pltpu.VMEM((NZ - 1, SLICE, KV), BF16),
-            pltpu.VMEM((2, TOK, KV), F32),
+            pltpu.VMEM((2, TOK, KV), BF16),
             pltpu.VMEM((ROWS, KV), F32),
             dma((5,)),
             dma((NX,)), dma((NX,)),

time: 48.4 us -> 47 us (0.971); the launches traced: 48.1 us -> 46.2 us
  Pallas kernels: 47.5 us -> 45.6 us
    pallas_call x1, Pallas kernels: 46 us -> 44.1 us  [per_device(): pl.pallas_call(exchange, out_shape=shapes, in_specs=[anywhere, vmem, anyw...]
where the time goes in v4:
time: 47 us; the launch traced here: 46.2 us
  Pallas kernels  45.6 us (97%)
  between operations  0.64 us (1%)
    pallas_call x1, Pallas kernels, per_device(): pl.pallas_call(exchange, out_shape=shapes, in_specs=[anywhere, vmem, anyw...  44.1 us
    pallas_call x1, Pallas kernels, per_device(): pl.pallas_call(store, out_shape=shapes, in_specs=[anywhere] * 5, out_spec...  1.49 us

profile of v4, /device:TPU:1, one launch (start us, length us, event | category | flops | bytes accessed | tf_op | source)
XLA Modules:
  0.0 46.2 jit_solution(15103728724051813410)
XLA Ops:
  0.6 44.1 %shard_map.101 = (bf16[128,4096]{1,0:T(8,128)(2,1)S(1)}, bf16[128,512]{1,0:T(8,128)(2,1)S(1)}, bf16[256,512]{1,0:T(8,128)(2,1)S(1)}, f32[256,512]{1,0:T(8,128)S(1)}, f32[256,512]{1,0:T(8,128)S(1)}) custom-call(bf16[128,4096]{1,0:T(8,128)(2,1)} %bitcast.7, bf16[1,4096]{1,0:T(2,128)(2,1)} %gain.1, bf16[128,512]{1,0:T(8,128)(2,1)} %bitcast.10, ...), custom_call_target="tpu_custom_call" | custom-call | tf_op jit(solution)/shard_map/pallas_call | solution.py:494
  44.7 1.5 %shard_map.102 = (bf16[128,4096]{1,0:T(8,128)(2,1)}, bf16[128,512]{1,0:T(8,128)(2,1)}, bf16[256,512]{1,0:T(8,128)(2,1)}, f32[256,512]{1,0:T(8,128)}, f32[256,512]{1,0:T(8,128)}) custom-call(bf16[128,4096]{1,0:T(8,128)(2,1)S(1)} %get-tuple-element.15.refs_0_, bf16[128,512]{1,0:T(8,128)(2,1)S(1)} %get-tuple-element.16.refs_1_, ...), custom_call_target="tpu_custom_call" | custom-call | tf_op jit(solution)/shard_map/pallas_call | solution.py:541

commit v5 on v4

--- a/solution.py
+++ b/solution.py
@@ -177,10 +177,12 @@
     squares = lax.fori_loop(0, 16, add_square, jnp.zeros((TOK, ROWS), F32))
     inv_v[...] = lax.rsqrt(jnp.sum(squares, axis=-1, keepdims=True) / D + EPSILON)
 
-    @pl.loop(0, 16)
-    def _(f):
-        scaled = h_v[:, columns(f)].astype(F32) * inv_v[...]
-        n_send[f] = (scaled * gain[:, columns(f)].astype(F32)).astype(BF16)
+    def make_normed(block):
+        @pl.loop(0, NX)
+        def _(part):
+            f = part * NY + block
+            scaled = h_v[:, columns(f)].astype(F32) * inv_v[...]
+            n_send[f] = (scaled * gain[:, columns(f)].astype(F32)).astype(BF16)
 
     @pl.when(z > 4)
     def _():
@@ -191,8 +193,15 @@
         def _():
             tell(above_sem, along_z(NZ - d))
 
+    loads[3].wait()
+    core_half.wait_recv()
+    q_send[...] = (d_own[...].astype(F32) + d_recv[...].astype(F32)).astype(BF16)
+    half_copy = remote(q_send, q_recv, c_ssem.at[1], c_rsem.at[1], other_half)
+    half_copy.start()
+
     n_copies = []
     for n, block in enumerate(order):
+        make_normed(block)
         for d in (1, 3, 2):
             copy = remote(
                 n_send.at[((i + d) % NX) * NY + block], n_buf.at[block, own_rows],
@@ -207,12 +216,6 @@
     for block in range(NY):
         n_buf[block, own_rows] = n_send[i * NY + block]
 
-    loads[3].wait()
-    core_half.wait_recv()
-    q_send[...] = (d_own[...].astype(F32) + d_recv[...].astype(F32)).astype(BF16)
-    half_copy = remote(q_send, q_recv, c_ssem.at[1], c_rsem.at[1], other_half)
-    half_copy.start()
-
     z_copies = [
         remote(
             p_send.at[slice_rows((z + d) % NZ)], z_recv.at[d - 1],
@@ -347,8 +350,8 @@
     await_weight(1)
     make_weight_grad(0)
     start_chain(0)
+    pl.when(late)(send_slices)
     send_grad(1)
-    pl.when(late)(send_slices)
     forward_weight(3, 1)
     make_weight_grad(1)
     start_chain(1)

time: 47 us -> 46.6 us (level); the launches traced: 46.2 us -> 46.4 us
  no operation moved by 1% of the time
where the time goes in v5:
time: 46.6 us; the launch traced here: 46.4 us
  Pallas kernels  45.7 us (98%)
  between operations  0.64 us (1%)
    pallas_call x1, Pallas kernels, per_device(): pl.pallas_call(exchange, out_shape=shapes, in_specs=[anywhere, vmem, anyw...  44.2 us
    pallas_call x1, Pallas kernels, per_device(): pl.pallas_call(store, out_shape=shapes, in_specs=[anywhere] * 5, out_spec...  1.49 us

profile of v5, /device:TPU:1, one launch (start us, length us, event | category | flops | bytes accessed | tf_op | source)
XLA Modules:
  0.0 46.4 jit_solution(2485080756992720266)
XLA Ops:
  0.6 44.2 %shard_map.101 = (bf16[128,4096]{1,0:T(8,128)(2,1)S(1)}, bf16[128,512]{1,0:T(8,128)(2,1)S(1)}, bf16[256,512]{1,0:T(8,128)(2,1)S(1)}, f32[256,512]{1,0:T(8,128)S(1)}, f32[256,512]{1,0:T(8,128)S(1)}) custom-call(bf16[128,4096]{1,0:T(8,128)(2,1)} %bitcast.7, bf16[1,4096]{1,0:T(2,128)(2,1)} %gain.1, bf16[128,512]{1,0:T(8,128)(2,1)} %bitcast.10, ...), custom_call_target="tpu_custom_call" | custom-call | tf_op jit(solution)/shard_map/pallas_call | solution.py:497
  44.9 1.5 %shard_map.102 = (bf16[128,4096]{1,0:T(8,128)(2,1)}, bf16[128,512]{1,0:T(8,128)(2,1)}, bf16[256,512]{1,0:T(8,128)(2,1)}, f32[256,512]{1,0:T(8,128)}, f32[256,512]{1,0:T(8,128)}) custom-call(bf16[128,4096]{1,0:T(8,128)(2,1)S(1)} %get-tuple-element.15.refs_0_, bf16[128,512]{1,0:T(8,128)(2,1)S(1)} %get-tuple-element.16.refs_1_, ...), custom_call_target="tpu_custom_call" | custom-call | tf_op jit(solution)/shard_map/pallas_call | solution.py:544

commit v6 on v5

--- a/solution.py
+++ b/solution.py
@@ -184,20 +184,22 @@
             scaled = h_v[:, columns(f)].astype(F32) * inv_v[...]
             n_send[f] = (scaled * gain[:, columns(f)].astype(F32)).astype(BF16)
 
-    @pl.when(z > 4)
-    def _():
-        pl.semaphore_wait(below_sem, 1)
-
-    for d in range(2, NZ):
-        @pl.when(jnp.logical_and(z >= d, z < d + 4))
-        def _():
-            tell(above_sem, along_z(NZ - d))
-
-    loads[3].wait()
-    core_half.wait_recv()
-    q_send[...] = (d_own[...].astype(F32) + d_recv[...].astype(F32)).astype(BF16)
-    half_copy = remote(q_send, q_recv, c_ssem.at[1], c_rsem.at[1], other_half)
-    half_copy.start()
+    def spread_word():
+        @pl.when(z > 4)
+        def _():
+            pl.semaphore_wait(below_sem, 1)
+
+        for d in range(2, NZ):
+            @pl.when(jnp.logical_and(z >= d, z < d + 4))
+            def _():
+                tell(above_sem, along_z(NZ - d))
+
+        loads[3].wait()
+        core_half.wait_recv()
+        q_send[...] = (d_own[...].astype(F32) + d_recv[...].astype(F32)).astype(BF16)
+        half_copy = remote(q_send, q_recv, c_ssem.at[1], c_rsem.at[1], other_half)
+        half_copy.start()
+        return half_copy
 
     n_copies = []
     for n, block in enumerate(order):
@@ -210,6 +212,7 @@
             copy.start()
             n_copies.append(copy)
         if n == 0:
+            half_copy = spread_word()
             for first, second in zip(vg_first, vg_second):
                 first.wait_recv()
                 second.start()

time: 46.6 us -> 46.6 us (level)
  no operation moved by 1% of the time
where the time goes in v6:
time: 46.6 us; the launch traced here: 46.4 us
  Pallas kernels  45.7 us (98%)
  between operations  0.64 us (1%)
    pallas_call x1, Pallas kernels, per_device(): pl.pallas_call(exchange, out_shape=shapes, in_specs=[anywhere, vmem, anyw...  44.2 us
    pallas_call x1, Pallas kernels, per_device(): pl.pallas_call(store, out_shape=shapes, in_specs=[anywhere] * 5, out_spec...  1.49 us

profile of v6, /device:TPU:1, one launch (start us, length us, event | category | flops | bytes accessed | tf_op | source)
XLA Modules:
  0.0 46.4 jit_solution(8687531918817076926)
XLA Ops:
  0.6 44.2 %shard_map.101 = (bf16[128,4096]{1,0:T(8,128)(2,1)S(1)}, bf16[128,512]{1,0:T(8,128)(2,1)S(1)}, bf16[256,512]{1,0:T(8,128)(2,1)S(1)}, f32[256,512]{1,0:T(8,128)S(1)}, f32[256,512]{1,0:T(8,128)S(1)}) custom-call(bf16[128,4096]{1,0:T(8,128)(2,1)} %bitcast.7, bf16[1,4096]{1,0:T(2,128)(2,1)} %gain.1, bf16[128,512]{1,0:T(8,128)(2,1)} %bitcast.10, ...), custom_call_target="tpu_custom_call" | custom-call | tf_op jit(solution)/shard_map/pallas_call | solution.py:500
  44.9 1.5 %shard_map.102 = (bf16[128,4096]{1,0:T(8,128)(2,1)}, bf16[128,512]{1,0:T(8,128)(2,1)}, bf16[256,512]{1,0:T(8,128)(2,1)}, f32[256,512]{1,0:T(8,128)}, f32[256,512]{1,0:T(8,128)}) custom-call(bf16[128,4096]{1,0:T(8,128)(2,1)S(1)} %get-tuple-element.15.refs_0_, bf16[128,512]{1,0:T(8,128)(2,1)S(1)} %get-tuple-element.16.refs_1_, ...), custom_call_target="tpu_custom_call" | custom-call | tf_op jit(solution)/shard_map/pallas_call | solution.py:547
